TPU v7x, 32 devices: a whole 2x2x4 slice. The times are simulated.
32 devices in a mesh: grp: 2 (over x), chan: 16 (over z, y, core).
Axes of the slice: x: 2, y: 2, z: 4, core: 2. Of those that a mesh axis runs over, the one named last changes fastest.
Arguments:
- voltages: bfloat16 [4096, 64, 512], P('chan', 'grp'), parts along dimension 1, may hold values from -6 to 6
- exponents: int32 [64], P('grp'), parts along dimension 0, may hold values from 0 to 2, as said below
- pairs: int32 [128, 2], replicated, may hold values from 0 to 31, as said below
Outputs:
- visibilities: bfloat16 [64, 128, 2, 128, 128], P(('grp', 'chan')), parts along dimension 0
There are 2 independent parts, one for each index of `grp`. A program takes and returns all parts, laid end to end along the dimension named above; an argument that names none is the same for every part. Nothing has to cross between parts.
Inputs may be any that keep to these rules, and one draw needn't show every extreme that they name: exponents are whole numbers. The 128 pairs are distinct and each has first member at most its second.
All inputs are finite; a program needn't handle non-finite values.
Results may differ from a plain program's by a relative error of at most 0.001.
Values may be sent and summed in bfloat16 or wider, within the bound.
A program may use at most 192 MiB of HBM per device.

v0:
```python
import jax
import jax.numpy as jnp
from jax import lax
from jax.sharding import PartitionSpec as P

PANEL = 128
NT = 256


def correlate_plane(plane, pairs):
    width = plane.shape[1]
    half = width // 2
    count = plane.shape[0] // PANEL
    panels = plane.reshape(count, PANEL, width)
    group_size = 32
    groups = pairs.reshape(-1, group_size, 2)
    labels = jnp.arange(count, dtype=jnp.int32)

    def select(which):
        onehot = (which[:, None] == labels[None, :]).astype(jnp.bfloat16)
        picked = jnp.einsum("kn,nix->kix", onehot, panels, preferred_element_type=jnp.float32)
        return picked.astype(jnp.bfloat16).reshape(group_size, PANEL, 2, half)

    def one_group(chosen):
        left = select(chosen[:, 0])
        right = select(chosen[:, 1])
        quads = jnp.einsum("kiat,kjbt->kabij", left, right, preferred_element_type=jnp.float32)
        real_part = quads[:, 0, 0] + quads[:, 1, 1]
        imag_part = quads[:, 1, 0] - quads[:, 0, 1]
        return jnp.stack([real_part, imag_part], axis=1)

    return lax.map(one_group, groups).reshape(-1, 2, PANEL, PANEL)


def correlate_channels(turned, pairs):

    def one_channel(plane):
        return correlate_plane(plane, pairs)

    return lax.map(one_channel, jnp.moveaxis(turned, 1, 0))


def input_power(turned):
    wide = turned.astype(jnp.float32)
    return jnp.sum(wide * wide, axis=(1, 2))


def on_device(voltages, exponents, pairs):
    gain = jnp.exp2(-exponents.astype(jnp.float32)).astype(jnp.bfloat16)
    scaled = voltages * gain[None, :, None]
    total_samples = exponents.shape[0] * NT
    power = lax.all_gather(input_power(scaled), "chan", axis=0, tiled=True)
    turned = lax.all_to_all(scaled, "chan", split_axis=1, concat_axis=0, tiled=True)
    raw = correlate_channels(turned, pairs)
    mean_power = power / total_samples
    rows = mean_power.reshape(-1, PANEL)
    left_power = jnp.take(rows, pairs[:, 0], axis=0)
    right_power = jnp.take(rows, pairs[:, 1], axis=0)
    denom = jnp.sqrt(NT * left_power[:, :, None] * right_power[:, None, :])
    return (raw / denom[None, :, None, :, :]).astype(jnp.bfloat16)


def solution(mesh):
    return jax.shard_map(
        on_device,
        mesh=mesh,
        in_specs=(P("chan", "grp", None), P("grp"), P()),
        out_specs=P(("grp", "chan"), None, None, None, None),
        check_vma=False,
    )
```

profile of v0, /device:TPU:11, one launch (start us, length us, event | category | flops | bytes accessed | tf_op | source)
XLA Modules:
  0.0 683.6 jit_solution(13939410700513925443)
XLA Ops:
  0.7 9.6 %multiply_reduce_fusion = (f32[256]{0:T(256)S(1)}, bf16[256,32,512]{2,0,1:T(8,128)(2,1)}) fusion(bf16[32]{0:T(256)(128)(2,1)S(1)} %exponential_convert_fusion, bf16[256,32,512]{2,1,0:T(8,128)(2,1)} %param.9), kind=kLoop, calls=%fused_computation.29 | loop fusion | flops 16776960 | bytes 16778304 | tf_op jit(solution)/shard_map/reduce_sum | solution.py:45
  17.1 192.6 %all-gather = f32[16,1,256]{2,1,0:T(1,128)S(1)} all-gather(f32[1,1,256]{2,1,0:T(1,128)S(1)} %bitcast.99), channel_id=1, replica_groups=mesh['grp'=2,'chan'=16] {'chan'}, dimensions={0}, use_global_device_ids=true | all-gather | bytes 17408 | tf_op jit(solution)/shard_map/all_gather | solution.py:52
  215.7 7.5 %copy.26 = bf16[16,256,2,512]{3,1,0,2:T(8,128)(2,1)} copy(bf16[16,256,2,512]{3,1,2,0:T(8,128)(2,1)} %bitcast.3) | data formatting | bytes 16777216 | tf_op jit(solution)/shard_map/all_to_all | solution.py:53
  223.2 440.5 %while.23 = (s32[]{:T(128)}, f32[2,128,2,128,128]{4,3,2,1,0:T(8,128)}, s32[128,2]{0,1:T(2,128)S(1)}, bf16[2,4096,512]{2,1,0:T(8,128)(2,1)}, s32[]{:T(128)}, /*index=5*/s32[]{:T(128)}, s32[]{:T(128)}) while((s32[]{:T(128)}, f32[2,128,2,128,128]{4,3,2,1,0:T(8,128)}, s32[128,2]{0,1:T(2,128)S(1)}, bf16[2,4096,512]{2,1,0:T(8,128)(2,1)}, s32[]{:T(128)}, ...), condition=%wide.region_3.4_spmd, body=%wide.region_0.3_spmd.sunk | while | flops 1348470784 | bytes 138415600 | solution.py:40
  230.2 201.7 %while.24 = (s32[]{:T(128)}, f32[4,32,2,128,128]{4,3,2,1,0:T(8,128)}, s32[4,32,2]{1,0,2:T(4,128)S(1)}, bf16[32,128,512]{2,0,1:T(8,128)(2,1)}, s32[]{:T(128)}) while((s32[]{:T(128)}, f32[4,32,2,128,128]{4,3,2,1,0:T(8,128)}, s32[4,32,2]{1,0,2:T(4,128)S(1)}, bf16[32,128,512]{2,0,1:T(8,128)(2,1)}, s32[]{:T(128)}) %tuple.52), condition=%wide.region_2.2_spmd.clone.clone, body=%wide.region_1.1_spmd.clone.clone.sunk | while | flops 1348470784 | bytes 88081744 | solution.py:32
  235.6 6.9 %reshape.106 = bf16[32,128,2,256]{3,2,0,1:T(2,128)(2,1)} reshape(bf16[32,128,512]{2,0,1:T(8,128)(2,1)} %convolution_convert_fusion.4) | data formatting | bytes 8388608 | tf_op jit(solution)/shard_map/while/body/eval_jaxpr/while/body/eval_jaxpr/reshape | solution.py:22
  248.0 6.9 %reshape.107 = bf16[32,128,2,256]{3,2,0,1:T(2,128)(2,1)} reshape(bf16[32,128,512]{2,0,1:T(8,128)(2,1)} %convolution_convert_fusion.5) | data formatting | bytes 8388608 | tf_op jit(solution)/shard_map/while/body/eval_jaxpr/while/body/eval_jaxpr/reshape | solution.py:22
  254.9 12.5 %fusion.36 = f32[32,2,2,128,128]{3,4,1,2,0:T(8,128)S(1)} fusion(bf16[32,128,2,256,1]{3,2,0,1,4:T(2,128)(2,1)} %bitcast.91, bf16[32,128,2,256,1]{3,2,0,1,4:T(2,128)(2,1)} %bitcast.92), kind=kOutput, calls=%fused_computation.7.clone.1 | convolution fusion | flops 1073741824 | bytes 16777216 | tf_op jit(solution)/shard_map/while/body/eval_jaxpr/while/body/eval_jaxpr/kiat,kjbt->kabij/dot_general | solution.py:27
  286.0 6.9 %reshape.106 = bf16[32,128,2,256]{3,2,0,1:T(2,128)(2,1)} reshape(bf16[32,128,512]{2,0,1:T(8,128)(2,1)} %convolution_convert_fusion.4) | data formatting | bytes 8388608 | tf_op jit(solution)/shard_map/while/body/eval_jaxpr/while/body/eval_jaxpr/reshape | solution.py:22
  298.4 6.9 %reshape.107 = bf16[32,128,2,256]{3,2,0,1:T(2,128)(2,1)} reshape(bf16[32,128,512]{2,0,1:T(8,128)(2,1)} %convolution_convert_fusion.5) | data formatting | bytes 8388608 | tf_op jit(solution)/shard_map/while/body/eval_jaxpr/while/body/eval_jaxpr/reshape | solution.py:22
  305.3 12.5 %fusion.36 = f32[32,2,2,128,128]{3,4,1,2,0:T(8,128)S(1)} fusion(bf16[32,128,2,256,1]{3,2,0,1,4:T(2,128)(2,1)} %bitcast.91, bf16[32,128,2,256,1]{3,2,0,1,4:T(2,128)(2,1)} %bitcast.92), kind=kOutput, calls=%fused_computation.7.clone.1 | convolution fusion | flops 1073741824 | bytes 16777216 | tf_op jit(solution)/shard_map/while/body/eval_jaxpr/while/body/eval_jaxpr/kiat,kjbt->kabij/dot_general | solution.py:27
  336.4 6.9 %reshape.106 = bf16[32,128,2,256]{3,2,0,1:T(2,128)(2,1)} reshape(bf16[32,128,512]{2,0,1:T(8,128)(2,1)} %convolution_convert_fusion.4) | data formatting | bytes 8388608 | tf_op jit(solution)/shard_map/while/body/eval_jaxpr/while/body/eval_jaxpr/reshape | solution.py:22
  348.8 6.9 %reshape.107 = bf16[32,128,2,256]{3,2,0,1:T(2,128)(2,1)} reshape(bf16[32,128,512]{2,0,1:T(8,128)(2,1)} %convolution_convert_fusion.5) | data formatting | bytes 8388608 | tf_op jit(solution)/shard_map/while/body/eval_jaxpr/while/body/eval_jaxpr/reshape | solution.py:22
  355.7 12.5 %fusion.36 = f32[32,2,2,128,128]{3,4,1,2,0:T(8,128)S(1)} fusion(bf16[32,128,2,256,1]{3,2,0,1,4:T(2,128)(2,1)} %bitcast.91, bf16[32,128,2,256,1]{3,2,0,1,4:T(2,128)(2,1)} %bitcast.92), kind=kOutput, calls=%fused_computation.7.clone.1 | convolution fusion | flops 1073741824 | bytes 16777216 | tf_op jit(solution)/shard_map/while/body/eval_jaxpr/while/body/eval_jaxpr/kiat,kjbt->kabij/dot_general | solution.py:27
  386.9 6.9 %reshape.106 = bf16[32,128,2,256]{3,2,0,1:T(2,128)(2,1)} reshape(bf16[32,128,512]{2,0,1:T(8,128)(2,1)} %convolution_convert_fusion.4) | data formatting | bytes 8388608 | tf_op jit(solution)/shard_map/while/body/eval_jaxpr/while/body/eval_jaxpr/reshape | solution.py:22
  399.2 6.9 %reshape.107 = bf16[32,128,2,256]{3,2,0,1:T(2,128)(2,1)} reshape(bf16[32,128,512]{2,0,1:T(8,128)(2,1)} %convolution_convert_fusion.5) | data formatting | bytes 8388608 | tf_op jit(solution)/shard_map/while/body/eval_jaxpr/while/body/eval_jaxpr/reshape | solution.py:22
  406.1 12.5 %fusion.36 = f32[32,2,2,128,128]{3,4,1,2,0:T(8,128)S(1)} fusion(bf16[32,128,2,256,1]{3,2,0,1,4:T(2,128)(2,1)} %bitcast.91, bf16[32,128,2,256,1]{3,2,0,1,4:T(2,128)(2,1)} %bitcast.92), kind=kOutput, calls=%fused_computation.7.clone.1 | convolution fusion | flops 1073741824 | bytes 16777216 | tf_op jit(solution)/shard_map/while/body/eval_jaxpr/while/body/eval_jaxpr/kiat,kjbt->kabij/dot_general | solution.py:27
  431.8 11.6 %bitcast_dynamic-update-slice_fusion.2 = f32[2,128,2,128,128]{4,3,2,1,0:T(8,128)} fusion(f32[2,128,2,128,128]{4,3,2,1,0:T(8,128)} %get-tuple-element.207, s32[]{:T(128)S(6)} %copy.66, f32[1,128,2,128,128]{4,3,2,1,0:T(8,128)} %bitcast.93), kind=kLoop, calls=%fused_computation.26.clone.1 | loop fusion | bytes 33554436 | tf_op jit(solution)/shard_map/while/body/jit(dynamic_update_index_in_dim)/dynamic_update_slice | solution.py:40
  450.5 201.6 %while.24 = (s32[]{:T(128)}, f32[4,32,2,128,128]{4,3,2,1,0:T(8,128)}, s32[4,32,2]{1,0,2:T(4,128)S(1)}, bf16[32,128,512]{2,0,1:T(8,128)(2,1)}, s32[]{:T(128)}) while((s32[]{:T(128)}, f32[4,32,2,128,128]{4,3,2,1,0:T(8,128)}, s32[4,32,2]{1,0,2:T(4,128)S(1)}, bf16[32,128,512]{2,0,1:T(8,128)(2,1)}, s32[]{:T(128)}) %tuple.52), condition=%wide.region_2.2_spmd.clone.clone, body=%wide.region_1.1_spmd.clone.clone.sunk | while | flops 1348470784 | bytes 88081744 | solution.py:32
  455.9 6.9 %reshape.106 = bf16[32,128,2,256]{3,2,0,1:T(2,128)(2,1)} reshape(bf16[32,128,512]{2,0,1:T(8,128)(2,1)} %convolution_convert_fusion.4) | data formatting | bytes 8388608 | tf_op jit(solution)/shard_map/while/body/eval_jaxpr/while/body/eval_jaxpr/reshape | solution.py:22
  468.3 6.9 %reshape.107 = bf16[32,128,2,256]{3,2,0,1:T(2,128)(2,1)} reshape(bf16[32,128,512]{2,0,1:T(8,128)(2,1)} %convolution_convert_fusion.5) | data formatting | bytes 8388608 | tf_op jit(solution)/shard_map/while/body/eval_jaxpr/while/body/eval_jaxpr/reshape | solution.py:22
  475.1 12.5 %fusion.36 = f32[32,2,2,128,128]{3,4,1,2,0:T(8,128)S(1)} fusion(bf16[32,128,2,256,1]{3,2,0,1,4:T(2,128)(2,1)} %bitcast.91, bf16[32,128,2,256,1]{3,2,0,1,4:T(2,128)(2,1)} %bitcast.92), kind=kOutput, calls=%fused_computation.7.clone.1 | convolution fusion | flops 1073741824 | bytes 16777216 | tf_op jit(solution)/shard_map/while/body/eval_jaxpr/while/body/eval_jaxpr/kiat,kjbt->kabij/dot_general | solution.py:27
  506.3 6.9 %reshape.106 = bf16[32,128,2,256]{3,2,0,1:T(2,128)(2,1)} reshape(bf16[32,128,512]{2,0,1:T(8,128)(2,1)} %convolution_convert_fusion.4) | data formatting | bytes 8388608 | tf_op jit(solution)/shard_map/while/body/eval_jaxpr/while/body/eval_jaxpr/reshape | solution.py:22
  518.7 6.9 %reshape.107 = bf16[32,128,2,256]{3,2,0,1:T(2,128)(2,1)} reshape(bf16[32,128,512]{2,0,1:T(8,128)(2,1)} %convolution_convert_fusion.5) | data formatting | bytes 8388608 | tf_op jit(solution)/shard_map/while/body/eval_jaxpr/while/body/eval_jaxpr/reshape | solution.py:22
  525.5 12.5 %fusion.36 = f32[32,2,2,128,128]{3,4,1,2,0:T(8,128)S(1)} fusion(bf16[32,128,2,256,1]{3,2,0,1,4:T(2,128)(2,1)} %bitcast.91, bf16[32,128,2,256,1]{3,2,0,1,4:T(2,128)(2,1)} %bitcast.92), kind=kOutput, calls=%fused_computation.7.clone.1 | convolution fusion | flops 1073741824 | bytes 16777216 | tf_op jit(solution)/shard_map/while/body/eval_jaxpr/while/body/eval_jaxpr/kiat,kjbt->kabij/dot_general | solution.py:27
  556.7 6.9 %reshape.106 = bf16[32,128,2,256]{3,2,0,1:T(2,128)(2,1)} reshape(bf16[32,128,512]{2,0,1:T(8,128)(2,1)} %convolution_convert_fusion.4) | data formatting | bytes 8388608 | tf_op jit(solution)/shard_map/while/body/eval_jaxpr/while/body/eval_jaxpr/reshape | solution.py:22
  569.1 6.9 %reshape.107 = bf16[32,128,2,256]{3,2,0,1:T(2,128)(2,1)} reshape(bf16[32,128,512]{2,0,1:T(8,128)(2,1)} %convolution_convert_fusion.5) | data formatting | bytes 8388608 | tf_op jit(solution)/shard_map/while/body/eval_jaxpr/while/body/eval_jaxpr/reshape | solution.py:22
  575.9 12.5 %fusion.36 = f32[32,2,2,128,128]{3,4,1,2,0:T(8,128)S(1)} fusion(bf16[32,128,2,256,1]{3,2,0,1,4:T(2,128)(2,1)} %bitcast.91, bf16[32,128,2,256,1]{3,2,0,1,4:T(2,128)(2,1)} %bitcast.92), kind=kOutput, calls=%fused_computation.7.clone.1 | convolution fusion | flops 1073741824 | bytes 16777216 | tf_op jit(solution)/shard_map/while/body/eval_jaxpr/while/body/eval_jaxpr/kiat,kjbt->kabij/dot_general | solution.py:27
  607.1 6.9 %reshape.106 = bf16[32,128,2,256]{3,2,0,1:T(2,128)(2,1)} reshape(bf16[32,128,512]{2,0,1:T(8,128)(2,1)} %convolution_convert_fusion.4) | data formatting | bytes 8388608 | tf_op jit(solution)/shard_map/while/body/eval_jaxpr/while/body/eval_jaxpr/reshape | solution.py:22
  626.3 12.5 %fusion.36 = f32[32,2,2,128,128]{3,4,1,2,0:T(8,128)S(1)} fusion(bf16[32,128,2,256,1]{3,2,0,1,4:T(2,128)(2,1)} %bitcast.91, bf16[32,128,2,256,1]{3,2,0,1,4:T(2,128)(2,1)} %bitcast.92), kind=kOutput, calls=%fused_computation.7.clone.1 | convolution fusion | flops 1073741824 | bytes 16777216 | tf_op jit(solution)/shard_map/while/body/eval_jaxpr/while/body/eval_jaxpr/kiat,kjbt->kabij/dot_general | solution.py:27
  652.1 11.6 %bitcast_dynamic-update-slice_fusion.2 = f32[2,128,2,128,128]{4,3,2,1,0:T(8,128)} fusion(f32[2,128,2,128,128]{4,3,2,1,0:T(8,128)} %get-tuple-element.207, s32[]{:T(128)S(6)} %copy.66, f32[1,128,2,128,128]{4,3,2,1,0:T(8,128)} %bitcast.93), kind=kLoop, calls=%fused_computation.26.clone.1 | loop fusion | bytes 33554436 | tf_op jit(solution)/shard_map/while/body/jit(dynamic_update_index_in_dim)/dynamic_update_slice | solution.py:40
  663.7 19.9 %divide_convert_fusion = bf16[2,128,2,128,128]{4,3,2,1,0:T(8,128)(2,1)} fusion(f32[2,128,2,128,128]{4,3,2,1,0:T(8,128)} %get-tuple-element.58, f32[128,128,128]{2,1,0:T(8,128)} %multiply_sqrt_fusion), kind=kLoop, calls=%fused_computation.28 | loop fusion | flops 16777216 | bytes 58720256 | tf_op jit(solution)/shard_map/convert_element_type | solution.py:60
  (95 shorter events, 226.6 us)
Async XLA Ops:
  10.3 199.4 %copy-start = (s32[128,2]{0,1:T(2,128)S(1)}, s32[128,2]{0,1:T(2,128)}, u32[]{:S(2)}) copy-start(s32[128,2]{0,1:T(2,128)} %param.11) | copy-start | bytes 3076
  10.3 205.4 %all-to-all-start = ((bf16[256,32,512]{2,0,1:T(8,128)(2,1)}), bf16[256,32,512]{2,0,1:T(8,128)(2,1)}, u32[]{:S(2)}, u32[]{:S(2)}) async-start(bf16[256,32,512]{2,0,1:T(8,128)(2,1)} %get-tuple-element.112), calls=%async_computation | async-start | bytes 16777216 | tf_op jit(solution)/shard_map/all_to_all | solution.py:53
where the time goes:
time: 688 us; the launch traced here: 684 us
  local copies, waits for them, and re-layouts  239 us (35%)
  blocking collectives  193 us (28%)
  matrix products  187 us (27%)
  other arithmetic  57.9 us (8%)
    all_gather x1, blocking collectives, on_device(): power = lax.all_gather(input_power(scaled), 'chan', axis=0, tiled=True)  193 us
    reshape x16, local copies, waits for them, and re-layouts, select(): return picked.astype(jnp.bfloat16).reshape(group_size, PANEL, 2, half)  111 us
    dot_general x8, matrix products, one_group(): jnp.einsum('kiat,kjbt->kabij', left, right, preferred_element_type=jnp.fl...  100 us
    dot_general x16, matrix products, select(): jnp.einsum('kn,nix->kix', onehot, panels, preferred_element_type=jnp.floa...  86.8 us
    dynamic_update_slice x16, local copies, waits for them, and re-layouts, correlate_plane(): return lax.map(one_group, groups).reshape(-1, 2, PANEL, PANEL)  82.5 us
    dynamic_update_slice x2, local copies, waits for them, and re-layouts, correlate_channels(): return lax.map(one_channel, jnp.moveaxis(turned, 1, 0))  23.3 us
    convert_element_type x1, other arithmetic, on_device(): return (raw / denom[None, :, None, :, :]).astype(jnp.bfloat16)  19.9 us
    broadcast_in_dim x8, other arithmetic, correlate_plane(): return lax.map(one_group, groups).reshape(-1, 2, PANEL, PANEL)  18 us
  transfers between devices with their start and end apart: 1, of which 0 were waited for; matrix products, arithmetic and copies ran while one was open for 1% of the time, Pallas kernels for 0%

commit v1 on v0

--- a/solution.py
+++ b/solution.py
@@ -50,7 +50,10 @@
     scaled = voltages * gain[None, :, None]
     total_samples = exponents.shape[0] * NT
     power = lax.all_gather(input_power(scaled), "chan", axis=0, tiled=True)
-    turned = lax.all_to_all(scaled, "chan", split_axis=1, concat_axis=0, tiled=True)
+    turned = jnp.concatenate(
+        lax.all_to_all(jnp.stack(jnp.split(scaled, lax.axis_size("chan"), axis=1)), "chan", 0, 0),
+        axis=0,
+    )
     raw = correlate_channels(turned, pairs)
     mean_power = power / total_samples
     rows = mean_power.reshape(-1, PANEL)

time: 688 us -> 723 us (1.051)
  local copies, waits for them, and re-layouts: 239 us -> 275 us
    unnamed x2 -> x19, local copies, waits for them, and re-layouts: 0.01 us -> 33.1 us
where the time goes in v1:
time: 723 us; the launch traced here: 719 us
  local copies, waits for them, and re-layouts  275 us (38%)
  blocking collectives  193 us (27%)
  matrix products  187 us (26%)
  other arithmetic  57.8 us (8%)
    all_gather x1, blocking collectives, on_device(): power = lax.all_gather(input_power(scaled), 'chan', axis=0, tiled=True)  193 us
    reshape x16, local copies, waits for them, and re-layouts, select(): return picked.astype(jnp.bfloat16).reshape(group_size, PANEL, 2, half)  111 us
    dot_general x8, matrix products, one_group(): jnp.einsum('kiat,kjbt->kabij', left, right, preferred_element_type=jnp.fl...  100 us
    dot_general x16, matrix products, select(): jnp.einsum('kn,nix->kix', onehot, panels, preferred_element_type=jnp.floa...  86.7 us
    dynamic_update_slice x16, local copies, waits for them, and re-layouts, correlate_plane(): return lax.map(one_group, groups).reshape(-1, 2, PANEL, PANEL)  82.4 us
    unnamed x19, local copies, waits for them, and re-layouts  33.1 us
    dynamic_update_slice x2, local copies, waits for them, and re-layouts, correlate_channels(): return lax.map(one_channel, jnp.moveaxis(turned, 1, 0))  23.3 us
    convert_element_type x1, other arithmetic, on_device(): return (raw / denom[None, :, None, :, :]).astype(jnp.bfloat16)  19.9 us
  transfers between devices with their start and end apart: 1, of which 0 were waited for; matrix products, arithmetic and copies ran while one was open for 1% of the time, Pallas kernels for 0%

profile of v1, /device:TPU:11, one launch (start us, length us, event | category | flops | bytes accessed | tf_op | source)
XLA Modules:
  0.0 718.9 jit_solution(2065897885350902417)
XLA Ops:
  0.7 9.5 %multiply_reduce_fusion = (f32[256]{0:T(256)S(1)}, bf16[256,32,512]{2,1,0:T(8,128)(2,1)}) fusion(bf16[256,32,512]{2,1,0:T(8,128)(2,1)} %param.9, bf16[32]{0:T(256)(128)(2,1)S(1)} %exponential_convert_fusion), kind=kLoop, calls=%fused_computation.29 | loop fusion | flops 16776960 | bytes 16778304 | tf_op jit(solution)/shard_map/reduce_sum | solution.py:45
  44.7 6.9 all-to-all-start
  51.6 192.6 %all-gather = f32[16,1,256]{2,1,0:T(1,128)S(1)} all-gather(f32[1,1,256]{2,1,0:T(1,128)S(1)} %bitcast.160), channel_id=1, replica_groups=mesh['grp'=2,'chan'=16] {'chan'}, dimensions={0}, use_global_device_ids=true | all-gather | bytes 17408 | tf_op jit(solution)/shard_map/all_gather | solution.py:52
  250.3 8.5 %copy.25 = bf16[16,256,2,512]{3,1,0,2:T(8,128)(2,1)} copy(bf16[16,256,2,512]{3,2,1,0:T(2,128)(2,1)} %all-to-all-done) | data formatting | bytes 16777216 | tf_op jit(solution)/shard_map/all_to_all | solution.py:54
  258.8 440.2 %while.23 = (s32[]{:T(128)}, f32[2,128,2,128,128]{4,3,2,1,0:T(8,128)}, s32[128,2]{0,1:T(2,128)S(1)}, bf16[2,4096,512]{2,1,0:T(8,128)(2,1)}, s32[]{:T(128)}, /*index=5*/s32[]{:T(128)}, s32[]{:T(128)}) while((s32[]{:T(128)}, f32[2,128,2,128,128]{4,3,2,1,0:T(8,128)}, s32[128,2]{0,1:T(2,128)S(1)}, bf16[2,4096,512]{2,1,0:T(8,128)(2,1)}, s32[]{:T(128)}, ...), condition=%wide.region_3.4_spmd, body=%wide.region_0.3_spmd.sunk | while | flops 1348470784 | bytes 138416592 | solution.py:40
  265.7 201.5 %while.24 = (s32[]{:T(128)}, f32[4,32,2,128,128]{4,3,2,1,0:T(8,128)}, s32[4,32,2]{1,0,2:T(4,128)S(1)}, bf16[32,128,512]{2,0,1:T(8,128)(2,1)}, s32[]{:T(128)}) while((s32[]{:T(128)}, f32[4,32,2,128,128]{4,3,2,1,0:T(8,128)}, s32[4,32,2]{1,0,2:T(4,128)S(1)}, bf16[32,128,512]{2,0,1:T(8,128)(2,1)}, s32[]{:T(128)}) %tuple.52), condition=%wide.region_2.2_spmd.clone.clone, body=%wide.region_1.1_spmd.clone.clone.sunk | while | flops 1348470784 | bytes 88082240 | solution.py:32
  271.2 6.9 reshape.110
  283.6 6.9 reshape.111
  290.5 12.5 %fusion.52 = f32[32,2,2,128,128]{3,4,1,2,0:T(8,128)S(1)} fusion(bf16[32,128,2,256,1]{3,2,0,1,4:T(2,128)(2,1)} %bitcast.152, bf16[32,128,2,256,1]{3,2,0,1,4:T(2,128)(2,1)} %bitcast.153), kind=kOutput, calls=%fused_computation.7.clone.1 | convolution fusion | flops 1073741824 | bytes 16777216 | tf_op jit(solution)/shard_map/while/body/eval_jaxpr/while/body/eval_jaxpr/kiat,kjbt->kabij/dot_general | solution.py:27
  321.6 6.9 reshape.110
  333.9 6.9 reshape.111
  340.8 12.5 %fusion.52 = f32[32,2,2,128,128]{3,4,1,2,0:T(8,128)S(1)} fusion(bf16[32,128,2,256,1]{3,2,0,1,4:T(2,128)(2,1)} %bitcast.152, bf16[32,128,2,256,1]{3,2,0,1,4:T(2,128)(2,1)} %bitcast.153), kind=kOutput, calls=%fused_computation.7.clone.1 | convolution fusion | flops 1073741824 | bytes 16777216 | tf_op jit(solution)/shard_map/while/body/eval_jaxpr/while/body/eval_jaxpr/kiat,kjbt->kabij/dot_general | solution.py:27
  371.9 6.9 reshape.110
  384.3 6.9 reshape.111
  391.2 12.5 %fusion.52 = f32[32,2,2,128,128]{3,4,1,2,0:T(8,128)S(1)} fusion(bf16[32,128,2,256,1]{3,2,0,1,4:T(2,128)(2,1)} %bitcast.152, bf16[32,128,2,256,1]{3,2,0,1,4:T(2,128)(2,1)} %bitcast.153), kind=kOutput, calls=%fused_computation.7.clone.1 | convolution fusion | flops 1073741824 | bytes 16777216 | tf_op jit(solution)/shard_map/while/body/eval_jaxpr/while/body/eval_jaxpr/kiat,kjbt->kabij/dot_general | solution.py:27
  422.3 6.9 reshape.110
  434.7 6.9 reshape.111
  441.6 12.5 %fusion.52 = f32[32,2,2,128,128]{3,4,1,2,0:T(8,128)S(1)} fusion(bf16[32,128,2,256,1]{3,2,0,1,4:T(2,128)(2,1)} %bitcast.152, bf16[32,128,2,256,1]{3,2,0,1,4:T(2,128)(2,1)} %bitcast.153), kind=kOutput, calls=%fused_computation.7.clone.1 | convolution fusion | flops 1073741824 | bytes 16777216 | tf_op jit(solution)/shard_map/while/body/eval_jaxpr/while/body/eval_jaxpr/kiat,kjbt->kabij/dot_general | solution.py:27
  467.3 11.6 %bitcast_dynamic-update-slice_fusion.2 = f32[2,128,2,128,128]{4,3,2,1,0:T(8,128)} fusion(f32[2,128,2,128,128]{4,3,2,1,0:T(8,128)} %get-tuple-element.207, s32[]{:T(128)} %get-tuple-element.206, f32[1,128,2,128,128]{4,3,2,1,0:T(8,128)} %bitcast.154), kind=kLoop, calls=%fused_computation.26.clone.1 | loop fusion | bytes 33554944 | tf_op jit(solution)/shard_map/while/body/jit(dynamic_update_index_in_dim)/dynamic_update_slice | solution.py:40
  485.9 201.5 %while.24 = (s32[]{:T(128)}, f32[4,32,2,128,128]{4,3,2,1,0:T(8,128)}, s32[4,32,2]{1,0,2:T(4,128)S(1)}, bf16[32,128,512]{2,0,1:T(8,128)(2,1)}, s32[]{:T(128)}) while((s32[]{:T(128)}, f32[4,32,2,128,128]{4,3,2,1,0:T(8,128)}, s32[4,32,2]{1,0,2:T(4,128)S(1)}, bf16[32,128,512]{2,0,1:T(8,128)(2,1)}, s32[]{:T(128)}) %tuple.52), condition=%wide.region_2.2_spmd.clone.clone, body=%wide.region_1.1_spmd.clone.clone.sunk | while | flops 1348470784 | bytes 88082240 | solution.py:32
  491.3 6.9 reshape.110
  503.7 6.9 reshape.111
  510.6 12.5 %fusion.52 = f32[32,2,2,128,128]{3,4,1,2,0:T(8,128)S(1)} fusion(bf16[32,128,2,256,1]{3,2,0,1,4:T(2,128)(2,1)} %bitcast.152, bf16[32,128,2,256,1]{3,2,0,1,4:T(2,128)(2,1)} %bitcast.153), kind=kOutput, calls=%fused_computation.7.clone.1 | convolution fusion | flops 1073741824 | bytes 16777216 | tf_op jit(solution)/shard_map/while/body/eval_jaxpr/while/body/eval_jaxpr/kiat,kjbt->kabij/dot_general | solution.py:27
  541.7 6.9 reshape.110
  560.9 12.5 %fusion.52 = f32[32,2,2,128,128]{3,4,1,2,0:T(8,128)S(1)} fusion(bf16[32,128,2,256,1]{3,2,0,1,4:T(2,128)(2,1)} %bitcast.152, bf16[32,128,2,256,1]{3,2,0,1,4:T(2,128)(2,1)} %bitcast.153), kind=kOutput, calls=%fused_computation.7.clone.1 | convolution fusion | flops 1073741824 | bytes 16777216 | tf_op jit(solution)/shard_map/while/body/eval_jaxpr/while/body/eval_jaxpr/kiat,kjbt->kabij/dot_general | solution.py:27
  592.1 6.9 reshape.110
  604.4 6.9 reshape.111
  611.3 12.5 %fusion.52 = f32[32,2,2,128,128]{3,4,1,2,0:T(8,128)S(1)} fusion(bf16[32,128,2,256,1]{3,2,0,1,4:T(2,128)(2,1)} %bitcast.152, bf16[32,128,2,256,1]{3,2,0,1,4:T(2,128)(2,1)} %bitcast.153), kind=kOutput, calls=%fused_computation.7.clone.1 | convolution fusion | flops 1073741824 | bytes 16777216 | tf_op jit(solution)/shard_map/while/body/eval_jaxpr/while/body/eval_jaxpr/kiat,kjbt->kabij/dot_general | solution.py:27
  642.4 6.9 reshape.110
  661.7 12.5 %fusion.52 = f32[32,2,2,128,128]{3,4,1,2,0:T(8,128)S(1)} fusion(bf16[32,128,2,256,1]{3,2,0,1,4:T(2,128)(2,1)} %bitcast.152, bf16[32,128,2,256,1]{3,2,0,1,4:T(2,128)(2,1)} %bitcast.153), kind=kOutput, calls=%fused_computation.7.clone.1 | convolution fusion | flops 1073741824 | bytes 16777216 | tf_op jit(solution)/shard_map/while/body/eval_jaxpr/while/body/eval_jaxpr/kiat,kjbt->kabij/dot_general | solution.py:27
  687.4 11.6 %bitcast_dynamic-update-slice_fusion.2 = f32[2,128,2,128,128]{4,3,2,1,0:T(8,128)} fusion(f32[2,128,2,128,128]{4,3,2,1,0:T(8,128)} %get-tuple-element.207, s32[]{:T(128)} %get-tuple-element.206, f32[1,128,2,128,128]{4,3,2,1,0:T(8,128)} %bitcast.154), kind=kLoop, calls=%fused_computation.26.clone.1 | loop fusion | bytes 33554944 | tf_op jit(solution)/shard_map/while/body/jit(dynamic_update_index_in_dim)/dynamic_update_slice | solution.py:40
  699.0 19.9 %divide_convert_fusion = bf16[2,128,2,128,128]{4,3,2,1,0:T(8,128)(2,1)} fusion(f32[2,128,2,128,128]{4,3,2,1,0:T(8,128)} %get-tuple-element.58, f32[128,128,128]{2,1,0:T(8,128)} %multiply_sqrt_fusion), kind=kLoop, calls=%fused_computation.28 | loop fusion | flops 16777216 | bytes 58720256 | tf_op jit(solution)/shard_map/convert_element_type | solution.py:63
  (113 shorter events, 261.1 us)
Async XLA Ops:
  10.2 23.5 %copy-start = (bf16[256,32,512]{2,1,0:T(8,128)(2,1)S(1)}, bf16[256,32,512]{2,1,0:T(8,128)(2,1)}, u32[]{:S(2)}) copy-start(bf16[256,32,512]{2,1,0:T(8,128)(2,1)} %get-tuple-element.112) | copy-start | bytes 25165828
  44.7 199.5 %copy-start.1 = (s32[128,2]{0,1:T(2,128)S(1)}, s32[128,2]{0,1:T(2,128)}, u32[]{:S(2)}) copy-start(s32[128,2]{0,1:T(2,128)} %param.11) | copy-start | bytes 3076
  44.7 205.6 %all-to-all-start = ((bf16[16,256,2,512]{3,2,1,0:T(2,128)(2,1)}), bf16[16,256,2,512]{3,2,1,0:T(2,128)(2,1)}, u32[]{:S(2)}, u32[]{:S(2)}) async-start(bf16[16,256,2,512]{3,2,1,0:T(2,128)(2,1)} %fusion.19), calls=%async_computation | async-start | bytes 16777216 | tf_op jit(solution)/shard_map/all_to_all | solution.py:54
